TPU v7x, 128 devices: a whole 4x4x4 slice. The times are simulated.
128 devices in a mesh: dp: 8 (over x, core), fsdp: 16 (over y, z).
Axes of the slice: x: 4, y: 4, z: 4, core: 2. Of those that a mesh axis runs over, the one named last changes fastest.
Arguments:
- rollout_hidden: bfloat16 [65536, 5120], P(('dp', 'fsdp')), may hold values from -64 to 64
- key_weight: bfloat16 [5120, 512], P('fsdp'), may hold values from -0.078125 to 0.078125
- value_weight: bfloat16 [5120, 512], P('fsdp'), may hold values from -0.078125 to 0.078125
- key_gain: float32 [128], replicated, may hold values from 0.1 to 1.9
- query_gain: float32 [128], replicated, may hold values from 0.1 to 1.9
- queries: bfloat16 [65536, 4096], P(('dp', 'fsdp')), may hold values from -64 to 64
- out_grad: bfloat16 [65536, 4096], P(('dp', 'fsdp')), may hold values from -6 to 6
- rewards: float32 [16, 8], P('fsdp'), may hold values from -4 to 4
- response_lengths: int32 [16, 8], P('fsdp'), may hold values from 256 to 512, as said below
- rollout_owner: int32 [16, 8], P('fsdp'), may hold values from 0 to 7, as said below
- train_shard: int32 [16, 8], P('fsdp'), may hold values from 0 to 7, as said below
- pack_offsets: int32 [16, 8], P('fsdp'), may hold values from 0 to 0, as said below
Outputs:
- d_hidden: bfloat16 [65536, 5120], P(('dp', 'fsdp'))
- d_queries: bfloat16 [65536, 4096], P(('dp', 'fsdp'))
- grad_key_weight: float32 [5120, 512], P('fsdp')
- grad_value_weight: float32 [5120, 512], P('fsdp')
- grad_query_gain: float32 [128], replicated
- grad_key_gain: float32 [128], replicated
Inputs may be any that keep to these rules, and one draw needn't show every extreme that they name: `response_lengths`: in every column at least one response is 512 long. `rollout_owner`: in every column each dp index generated exactly one response, and no two responses of a column generated by different dp indices go to the same training shard. `train_shard`: in every column each dp index trains exactly 1 responses. `pack_offsets`: multiples of 512; the responses that one dp index trains in one column have distinct offsets.
All inputs are finite; a program needn't handle non-finite values.
Results may differ from a plain program's by a relative error of at most 0.03.
Values may be sent and summed in bfloat16 or wider, within the bound.
A program may use at most 256 MiB of HBM per device.

v0:
```python
import math

import jax
import jax.numpy as jnp
from jax import lax
from jax.sharding import PartitionSpec as P

HD = 128
GSIZE = 4
TILE = 512


eps_norm = 1e-06
rope_base = 1000000.0


def rope_tables(length, head_width):
    half_width = head_width // 2
    position = jnp.arange(length).astype(jnp.float32)
    frequency = rope_base ** (-jnp.arange(half_width).astype(jnp.float32) / half_width)
    angles = position[:, None] * frequency[None, :]
    return (jnp.cos(angles)[:, None, :], jnp.sin(angles)[:, None, :])


def rotate(vectors, cosine, sine_table):
    half_width = vectors.shape[-1] // 2
    first_half = vectors[..., :half_width]
    second_half = vectors[..., half_width:]
    return jnp.concatenate(
        [
            first_half * cosine - second_half * sine_table,
            second_half * cosine + first_half * sine_table,
        ],
        axis=-1,
    )


def unrotate(gradients, cosine, sine_table):
    half_width = gradients.shape[-1] // 2
    first_half = gradients[..., :half_width]
    second_half = gradients[..., half_width:]
    return jnp.concatenate(
        [
            first_half * cosine + second_half * sine_table,
            second_half * cosine - first_half * sine_table,
        ],
        axis=-1,
    )


def norm_forward(raw_values, gain_vector):
    inv_scale = lax.rsqrt(jnp.mean(raw_values * raw_values, axis=-1, keepdims=True) + eps_norm)
    unit_rows = raw_values * inv_scale
    return (unit_rows * gain_vector, unit_rows, inv_scale)


def norm_backward(grad_out, unit_rows, inv_scale, gain_vector):
    grad_unit = grad_out * gain_vector
    grad_in = inv_scale * (
        grad_unit - unit_rows * jnp.mean(grad_unit * unit_rows, axis=-1, keepdims=True)
    )
    gain_part = jnp.sum((grad_out * unit_rows).reshape(-1, unit_rows.shape[-1]), axis=0)
    return (grad_in, gain_part)


def earlier_equal(labels):
    order_index = jnp.arange(labels.shape[-1])
    earlier = order_index[None, :] < order_index[:, None]
    same_label = (labels[:, None] == labels[None, :]) & earlier
    return jnp.sum(same_label.astype(jnp.int32), axis=-1)


def select_sum(selection, labels):
    return jnp.sum(selection.astype(jnp.int32) * labels[None, :], axis=1)


def pick_tiles(tile_stack, tile_index, live_tiles):
    picked = jnp.take(tile_stack, tile_index, axis=0)
    return jnp.where(live_tiles[:, None, None], picked, jnp.zeros_like(picked))


def attend_head(query_rot, key_tiles, value_tiles, scaled, allowed):
    inv_root = 1.0 / math.sqrt(key_tiles.shape[-1])
    scores = (
        jnp.einsum("bigd,bjd->bgij", query_rot, key_tiles, preferred_element_type=jnp.float32)
        * inv_root
    )
    weight = jnp.where(allowed[:, None], jnp.exp(scores), 0.0)
    probability = weight / jnp.sum(weight, axis=-1, keepdims=True)
    probs_low = probability.astype(jnp.bfloat16)
    attended = jnp.einsum(
        "bgij,bjd->bigd", probs_low, value_tiles, preferred_element_type=jnp.float32
    ).astype(jnp.bfloat16)
    grad_values = jnp.einsum(
        "bgij,bigd->bjd", probs_low, scaled, preferred_element_type=jnp.float32
    ).astype(jnp.bfloat16)
    grad_probs = jnp.einsum(
        "bigd,bjd->bgij", scaled, value_tiles, preferred_element_type=jnp.float32
    )
    dotted = jnp.einsum("bigd,bigd->bgi", scaled, attended, preferred_element_type=jnp.float32)
    grad_scores = (probability * (grad_probs - dotted[..., None])).astype(jnp.bfloat16)
    grad_query = (
        jnp.einsum("bgij,bjd->bigd", grad_scores, key_tiles, preferred_element_type=jnp.float32)
        * inv_root
    )
    grad_keys = (
        jnp.einsum("bgij,bigd->bjd", grad_scores, query_rot, preferred_element_type=jnp.float32)
        * inv_root
    ).astype(jnp.bfloat16)
    return (grad_query, grad_keys, grad_values)


def attend(query_rot, key_tiles, value_tiles, scaled, lengths):
    tile_rows = key_tiles.shape[1]
    row_index = jnp.arange(tile_rows)
    causal = row_index[None, :] <= row_index[:, None]
    allowed = causal[None] & (row_index[None, None, :] < lengths[:, None, None])

    def one_head(entry):
        query_head, key_head, value_head, scaled_head = entry
        return attend_head(query_head, key_head, value_head, scaled_head, allowed)

    heads_first = (
        jnp.moveaxis(query_rot, 2, 0),
        jnp.moveaxis(key_tiles, 2, 0),
        jnp.moveaxis(value_tiles, 2, 0),
        jnp.moveaxis(scaled, 2, 0),
    )
    grad_query, grad_keys, grad_values = lax.map(one_head, heads_first)
    return (
        jnp.moveaxis(grad_query, 0, 2),
        jnp.moveaxis(grad_keys, 0, 2),
        jnp.moveaxis(grad_values, 0, 2),
    )


def per_device(
    rollout_hidden,
    key_weight,
    value_weight,
    key_gain,
    query_gain,
    queries,
    out_grad,
    rewards,
    response_lengths,
    rollout_owner,
    train_shard,
    pack_offsets,
):
    groups = lax.axis_size("dp")
    dp_index = lax.axis_index("dp")
    lengths = response_lengths[0]
    owners = rollout_owner[0]
    trainers = train_shard[0]
    offsets = pack_offsets[0]
    tok_rows = rollout_hidden.shape[0]
    tile_rows = TILE
    slot_count = tok_rows // tile_rows
    pair_tiles = (slot_count + groups - 1) // groups
    kv_width = key_weight.shape[1]
    kv_heads = kv_width // HD
    query_heads = queries.shape[1] // HD
    group_size = query_heads // kv_heads
    cosine, sine_table = rope_tables(tile_rows, HD)
    own_rank = earlier_equal(owners)
    pair_rank = earlier_equal(owners * groups + trainers)
    pack_slot = offsets // tile_rows
    grouped = rewards[0].reshape(-1, GSIZE)
    advantage = (grouped - jnp.mean(grouped, axis=-1, keepdims=True)).reshape(-1)
    full_key, full_value = (
        lax.all_gather(key_weight, "fsdp", axis=0, tiled=True),
        lax.all_gather(value_weight, "fsdp", axis=0, tiled=True),
    )
    key_raw = jnp.dot(rollout_hidden, full_key, preferred_element_type=jnp.float32)
    value_rows = jnp.dot(rollout_hidden, full_value, preferred_element_type=jnp.float32).astype(
        jnp.bfloat16
    )
    key_normed, key_unit, key_inv = norm_forward(
        key_raw.reshape(slot_count, tile_rows, kv_heads, HD), key_gain
    )
    key_rot = (
        rotate(key_normed, cosine, sine_table)
        .astype(jnp.bfloat16)
        .reshape(slot_count, tile_rows, kv_width)
    )
    value_tiles = value_rows.reshape(slot_count, tile_rows, kv_width)
    slot_ids = jnp.arange(slot_count)
    pack_select = (trainers == dp_index)[None, :] & (pack_slot[None, :] == slot_ids[:, None])
    pack_lengths = select_sum(pack_select, lengths)
    pack_coef = jnp.sum(jnp.where(pack_select, advantage[None, :], 0.0), axis=1)
    pack_owner = select_sum(pack_select, owners)
    pack_pair = select_sum(pack_select, pair_rank)
    owned = owners == dp_index
    tile_select = owned[None, :] & (own_rank[None, :] == slot_ids[:, None])
    tile_trainer = select_sum(tile_select, trainers)
    tile_pair = select_sum(tile_select, pair_rank)
    peer_slot = jnp.arange(groups * pair_tiles)
    peer_index = peer_slot // pair_tiles
    rank_in = peer_slot % pair_tiles
    send_select = (
        owned[None, :]
        & (trainers[None, :] == peer_index[:, None])
        & (pair_rank[None, :] == rank_in[:, None])
    )
    send_tile = select_sum(send_select, own_rank)
    send_live = jnp.any(send_select, axis=1)
    back_select = (
        (trainers == dp_index)[None, :]
        & (owners[None, :] == peer_index[:, None])
        & (pair_rank[None, :] == rank_in[:, None])
    )
    back_tile = select_sum(back_select, pack_slot)
    back_live = jnp.any(back_select, axis=1)
    incoming_keys, incoming_values = (
        lax.all_to_all(
            pick_tiles(key_rot, send_tile, send_live), "dp", split_axis=0, concat_axis=0, tiled=True
        ),
        lax.all_to_all(
            pick_tiles(value_tiles, send_tile, send_live),
            "dp",
            split_axis=0,
            concat_axis=0,
            tiled=True,
        ),
    )
    source = pack_owner * pair_tiles + pack_pair
    pack_keys = jnp.take(incoming_keys, source, axis=0)
    pack_values = jnp.take(incoming_values, source, axis=0)
    query_raw = queries.reshape(slot_count, tile_rows, query_heads, HD).astype(jnp.float32)
    query_normed, query_unit, query_inv = norm_forward(query_raw, query_gain)
    query_rot = (
        rotate(query_normed, cosine, sine_table)
        .astype(jnp.bfloat16)
        .reshape(slot_count, tile_rows, kv_heads, group_size, HD)
    )
    row_index = jnp.arange(tile_rows)
    live_rows = (row_index[None, :] < pack_lengths[:, None]).astype(jnp.float32)
    row_coef = (pack_coef[:, None] * live_rows)[:, :, None, None]
    scaled = (
        row_coef * out_grad.reshape(slot_count, tile_rows, query_heads, HD).astype(jnp.float32)
    ).astype(jnp.bfloat16)
    scaled = scaled.reshape(slot_count, tile_rows, kv_heads, group_size, HD)
    grad_query, grad_keys, grad_values = attend(
        query_rot,
        pack_keys.reshape(slot_count, tile_rows, kv_heads, HD),
        pack_values.reshape(slot_count, tile_rows, kv_heads, HD),
        scaled,
        pack_lengths,
    )
    grad_query_normed = unrotate(
        grad_query.reshape(slot_count, tile_rows, query_heads, HD), cosine, sine_table
    )
    grad_query_raw, query_part = norm_backward(grad_query_normed, query_unit, query_inv, query_gain)
    d_queries = grad_query_raw.reshape(tok_rows, query_heads * HD).astype(jnp.bfloat16)
    grad_key_pack = grad_keys.reshape(slot_count, tile_rows, kv_width)
    grad_value_pack = grad_values.reshape(slot_count, tile_rows, kv_width)
    returned_keys, returned_values = (
        lax.all_to_all(
            pick_tiles(grad_key_pack, back_tile, back_live),
            "dp",
            split_axis=0,
            concat_axis=0,
            tiled=True,
        ),
        lax.all_to_all(
            pick_tiles(grad_value_pack, back_tile, back_live),
            "dp",
            split_axis=0,
            concat_axis=0,
            tiled=True,
        ),
    )
    source_back = tile_trainer * pair_tiles + tile_pair
    owner_key_grad = jnp.take(returned_keys, source_back, axis=0)
    owner_value_grad = jnp.take(returned_values, source_back, axis=0)
    value_grad_rows = owner_value_grad.reshape(tok_rows, kv_width)
    contract_rows = (((0,), (0,)), ((), ()))
    contract_cols = (((1,), (1,)), ((), ()))
    key_normed_grad = unrotate(
        owner_key_grad.reshape(slot_count, tile_rows, kv_heads, HD).astype(jnp.float32),
        cosine,
        sine_table,
    )
    key_raw_grad, key_part = norm_backward(key_normed_grad, key_unit, key_inv, key_gain)
    key_grad_rows = key_raw_grad.reshape(tok_rows, kv_width).astype(jnp.bfloat16)
    key_weight_part = lax.dot_general(
        rollout_hidden, key_grad_rows, contract_rows, preferred_element_type=jnp.float32
    )
    value_part = lax.dot_general(
        rollout_hidden, value_grad_rows, contract_rows, preferred_element_type=jnp.float32
    )
    key_shard, value_shard = (
        lax.psum_scatter(key_weight_part, "fsdp", scatter_dimension=0, tiled=True),
        lax.psum_scatter(value_part, "fsdp", scatter_dimension=0, tiled=True),
    )
    d_hidden = (
        lax.dot_general(key_grad_rows, full_key, contract_cols, preferred_element_type=jnp.float32)
        + lax.dot_general(
            value_grad_rows, full_value, contract_cols, preferred_element_type=jnp.float32
        )
    ).astype(jnp.bfloat16)
    grad_key_weight, grad_value_weight = lax.psum((key_shard, value_shard), "dp")
    grad_query_gain, grad_key_gain = lax.psum((query_part, key_part), ("dp", "fsdp"))
    return (d_hidden, d_queries, grad_key_weight, grad_value_weight, grad_query_gain, grad_key_gain)


def solution(mesh):
    in_specs = (
        P(("dp", "fsdp"), None),
        P("fsdp", None),
        P("fsdp", None),
        P(),
        P(),
        P(("dp", "fsdp"), None),
        P(("dp", "fsdp"), None),
        P("fsdp", None),
        P("fsdp", None),
        P("fsdp", None),
        P("fsdp", None),
        P("fsdp", None),
    )
    out_specs = (
        P(("dp", "fsdp"), None),
        P(("dp", "fsdp"), None),
        P("fsdp", None),
        P("fsdp", None),
        P(),
        P(),
    )
    return jax.shard_map(
        per_device, mesh=mesh, in_specs=in_specs, out_specs=out_specs, check_vma=False
    )
```

profile of v0, /device:TPU:1, one launch (start us, length us, event | category | flops | bytes accessed | tf_op | source)
XLA Modules:
  0.0 829.3 jit_solution(4391083761717655604)
XLA Ops:
  18.3 51.6 %all-gather.3.cloned.1.call-done = bf16[5120,512]{1,0:T(8,128)(2,1)} async-done(((bf16[320,512]{1,0:T(8,128)(2,1)}), bf16[5120,512]{1,0:T(8,128)(2,1)}) %all-gather.3.cloned.1.call-update) | async-done | bytes 5242896 | tf_op jit(solution)/shard_map/all_gather | solution.py:172
  81.5 46.7 %all-gather.5.cloned.1.call-done = bf16[5120,512]{1,0:T(8,128)(2,1)} async-done(((bf16[320,512]{1,0:T(8,128)(2,1)}), bf16[5120,512]{1,0:T(8,128)(2,1)}) %all-gather.5.cloned.1.call-update) | async-done | bytes 5242896 | tf_op jit(solution)/shard_map/all_gather | solution.py:173
  128.2 7.7 convolution_convert_fusion
  150.0 46.9 %all-to-all-done = bf16[8,512,512]{1,2,0:T(8,128)(2,1)} async-done(((bf16[8,512,512]{1,2,0:T(8,128)(2,1)}), bf16[8,512,512]{1,2,0:T(8,128)(2,1)}, u32[]{:S(2)}, u32[]{:S(2)}) %all-to-all-start) | async-done | bytes 4194336 | tf_op jit(solution)/shard_map/all_to_all | solution.py:216
  253.2 152.5 %while.16 = (s32[]{:T(128)}, f32[4,1,512,8,128]{2,4,3,1,0:T(8,128)}, bf16[4,1,512,128]{2,3,0,1:T(8,128)(2,1)}, bf16[4,1,512,128]{2,3,0,1:T(8,128)(2,1)}, bf16[4,...) while((s32[]{:T(128)}, ...), condition=%wide.region_14.17_spmd.clone, body=%wide.region_12.16_spmd.clone.sunk | while | flops 3260735488 | bytes 94474944 | solution.py:129
  253.3 6.6 fusion.128
  417.5 47.7 %all-to-all-done.2 = bf16[8,512,512]{1,2,0:T(8,128)(2,1)} async-done(((bf16[8,512,512]{1,2,0:T(8,128)(2,1)}), bf16[8,512,512]{1,2,0:T(8,128)(2,1)}, u32[]{:S(2)}, u32[]{:S(2)}) %all-to-all-start.2) | async-done | bytes 4194336 | tf_op jit(solution)/shard_map/all_to_all | solution.py:259
  482.8 7.9 convolution_bitcast_fusion.2
  490.6 11.4 %copy.146 = f32[5120,512]{1,0:T(8,128)} copy(f32[5120,512]{0,1:T(8,128)} %convolution_bitcast_fusion.2) | data formatting | bytes 20971520
  502.1 53.8 %all_to_all.20 = bf16[8,512,512]{1,2,0:T(8,128)(2,1)S(1)} all-to-all(bf16[8,512,512]{1,2,0:T(8,128)(2,1)} %get-tuple-element.214), channel_id=1, replica_groups=mesh['dp'=8,'fsdp'=16] {'dp'}, dimensions={0} | all-to-all | bytes 8388608 | tf_op jit(solution)/shard_map/all_to_all | solution.py:266
  557.8 8.0 convolution_bitcast_fusion.1
  565.8 11.3 %copy.148 = f32[5120,512]{1,0:T(8,128)} copy(f32[5120,512]{0,1:T(8,128)} %convolution_bitcast_fusion.1) | data formatting | bytes 20971520
  578.2 8.2 reshape.712
  590.2 8.7 %fusion.86 = (f32[1,512,32,64]{1,3,2,0:T(8,128)}, f32[1,512,32,64]{1,3,2,0:T(8,128)}) fusion(f32[1,512,32,128]{1,3,2,0:T(8,128)} %bitcast.341), kind=kLoop, calls=%fused_computation.162 | loop fusion | bytes 16777216 | tf_op jit(solution)/shard_map/slice | solution.py:41
  598.9 9.1 %copy.159 = f32[1,512,32,64]{3,2,1,0:T(8,128)} copy(f32[1,512,32,64]{1,3,2,0:T(8,128)} %get-tuple-element.205) | data formatting | bytes 8388608
  608.0 9.2 %copy.160 = f32[1,512,32,64]{3,2,1,0:T(8,128)} copy(f32[1,512,32,64]{1,3,2,0:T(8,128)} %get-tuple-element.204) | data formatting | bytes 8388608
  617.2 7.7 multiply_add_fusion
  624.8 18.5 %multiply_reduce_fusion.1 = (f32[512,32]{1,0:T(8,128)S(1)}, f32[1,512,32,128]{3,2,1,0:T(8,128)}) fusion(f32[128]{0:T(128)S(1)} %copy-done.27, f32[512,32]{1,0:T(8,128)S(1)} %copy-done.17, f32[1,512,32,64]{3,2,1,0:T(8,128)S(1)} %get-tuple-element.201, f32[1,512,32,64]{3,2,1,0:T(8,128)S(1)} %get-tuple-element.200, f32[1,512,32,128]{3,2,1,0:T(8,128)} %bitcast.328), kind=kLoop, calls=%fused_computation.66 | loop fusion | flops 10469376 | bytes 25297408 | tf_op jit(solution)/shard_map/reduce_sum | solution.py:60
  643.4 8.6 %fusion.60 = f32[128]{0:T(128)S(1)} fusion(f32[16384,64]{1,0:T(8,128)S(1)} %bitcast.330, f32[16384,64]{1,0:T(8,128)S(1)} %bitcast.329, f32[16384,128]{1,0:T(8,128)} %reshape.712, f32[16384]{0:T(1024)S(1)} %rsqrt.26), kind=kLoop, calls=%fused_computation.63 | loop fusion | flops 8388480 | bytes 16843264 | tf_op jit(solution)/shard_map/reduce_sum | solution.py:62
  659.9 21.2 %fusion.58 = bf16[512,4096]{1,0:T(8,128)(2,1)} fusion(f32[64,8,32,128]{3,2,1,0:T(8,128)S(1)} %bitcast.332, f32[64,8,32,128]{3,2,1,0:T(8,128)} %bitcast.331, f32[64,8,32,128]{3,2,1,0:T(8,128)} %bitcast.333, bf16[512,4096]{1,0:T(8,128)(2,1)S(1)} %copy-done.4, f32[4096]{0:T(1024)S(1)} %broadcast_bitcast_fusion), kind=kLoop, calls=%fused_computation.55 | loop fusion | flops 14680064 | bytes 33570816 | tf_op jit(solution)/shard_map/convert_element_type | solution.py:255
  681.8 64.8 %all-reduce = (f32[128]{0:T(128)}, f32[128]{0:T(128)}) all-reduce(f32[128]{0:T(128)S(1)} %fusion.60, f32[128]{0:T(128)S(1)} %fusion.67), channel_id=1, replica_groups=mesh['dp'=8,'fsdp'=16] {'dp','fsdp'}, use_global_device_ids=true, to_apply=%region_25.28 | all-reduce | flops 256 | bytes 2048 | tf_op jit(solution)/shard_map/psum | solution.py:304
  746.6 7.9 fusion.89
  759.1 11.2 %add_convert_fusion = bf16[512,5120]{1,0:T(8,128)(2,1)} fusion(f32[512,5120]{1,0:T(8,128)} %fusion.89, bf16[5120,512]{1,0:T(8,128)(2,1)} %all-gather.5.cloned.1.call-done, bf16[8,512,512]{1,2,0:T(8,128)(2,1)} %copy-done.18, s32[]{:T(128)} %bitcast.34, pred[]{:T(512)} %bitcast.10), kind=kOutput, calls=%fused_computation.51 | convolution fusion | flops 2689859584 | bytes 21496832 | tf_op jit(solution)/shard_map/dot_general | solution.py:299
  770.2 47.6 %all-reduce.4.cloned.1.call-done = (f32[320,512]{0,1:T(8,128)}, f32[320,512]{0,1:T(8,128)}) async-done(((f32[320,512]{0,1:T(8,128)}, f32[320,512]{0,1:T(8,128)}), (f32[320,512]{0,1:T(8,128)}, f32[320,512]{0,1:T(8,128)})) %all-reduce.4.cloned.1.call-update) | async-done | bytes 1310736 | tf_op jit(solution)/shard_map/psum | solution.py:303
  (230 shorter events, 289.6 us)
Async XLA Ops:
  7.2 62.7 %all-gather.3.cloned.1.call-start = ((), (), s32[]{:S(2)}) async-start(), calls=%async_computation.6 | async-start | bytes 5570560 | tf_op jit(solution)/shard_map/all_gather | solution.py:172
  7.9 120.3 %all-gather.5.cloned.1.call-start = ((), (), s32[]{:S(2)}) async-start(), calls=%async_computation.7 | async-start | bytes 5570560 | tf_op jit(solution)/shard_map/all_gather | solution.py:173
  18.3 197.8 %copy-start.12 = (f32[512,64]{1,0:T(8,128)}, f32[512,64]{1,0:T(8,128)S(1)}, u32[]{:S(2)}) copy-start(f32[512,64]{1,0:T(8,128)S(1)} %get-tuple-element.212) | copy-start | bytes 393220
  18.3 197.8 %copy-start.14 = (f32[512,64]{1,0:T(8,128)}, f32[512,64]{1,0:T(8,128)S(1)}, u32[]{:S(2)}) copy-start(f32[512,64]{1,0:T(8,128)S(1)} %get-tuple-element.213) | copy-start | bytes 393220
  18.3 58.8 %copy-start.28 = (f32[128]{0:T(128)S(1)}, f32[128]{0:T(128)}, u32[]{:S(2)}) copy-start(f32[128]{0:T(128)} %param.21) | copy-start | bytes 1540
  76.4 59.5 %copy-start.6 = (f32[512,512]{0,1:T(8,128)}, f32[512,512]{0,1:T(8,128)S(1)}, u32[]{:S(2)}) copy-start(f32[512,512]{0,1:T(8,128)S(1)} %fusion.88) | copy-start | bytes 3145732
  76.8 59.1 %copy-start.8 = (f32[1,512,4,128]{3,2,1,0:T(4,128)}, f32[1,512,4,128]{3,2,1,0:T(4,128)S(1)}, u32[]{:S(2)}) copy-start(f32[1,512,4,128]{3,2,1,0:T(4,128)S(1)} %copy.112) | copy-start | bytes 3145732
  77.1 58.8 %copy-start.19 = (f32[512,4]{1,0:T(8,128)}, f32[512,4]{1,0:T(8,128)S(1)}, u32[]{:S(2)}) copy-start(f32[512,4]{1,0:T(8,128)S(1)} %copy.111) | copy-start | bytes 24580
  138.0 10.0 %copy-start.32 = (s32[1,8]{1,0:T(1,128)S(1)}, s32[1,8]{1,0:T(1,128)}, u32[]{:S(2)}) copy-start(s32[1,8]{1,0:T(1,128)} %param.26) | copy-start | bytes 100
  142.8 54.0 %all-to-all-start = ((bf16[8,512,512]{1,2,0:T(8,128)(2,1)}), bf16[8,512,512]{1,2,0:T(8,128)(2,1)}, u32[]{:S(2)}, u32[]{:S(2)}) async-start(bf16[8,512,512]{1,2,0:T(8,128)(2,1)} %get-tuple-element.217), calls=%async_computation | async-start | bytes 8388608 | tf_op jit(solution)/shard_map/all_to_all | solution.py:216
  196.9 54.4 %all-to-all-start.1 = ((bf16[8,512,512]{1,2,0:T(8,128)(2,1)}), bf16[8,512,512]{1,2,0:T(8,128)(2,1)}, u32[]{:S(2)}, u32[]{:S(2)}) async-start(bf16[8,512,512]{1,2,0:T(8,128)(2,1)} %get-tuple-element.216), calls=%async_computation.1 | async-start | bytes 8388608 | tf_op jit(solution)/shard_map/all_to_all | solution.py:219
  253.2 152.5 %copy-start.30 = (pred[8]{0:T(512)(128)(4,1)S(1)}, pred[8]{0:T(512)(128)(4,1)}, u32[]{:S(2)}) copy-start(pred[8]{0:T(512)(128)(4,1)} %get-tuple-element.164) | copy-start | bytes 28
  253.2 152.5 %copy-start.31 = (pred[8]{0:T(512)(128)(4,1)S(1)}, pred[8]{0:T(512)(128)(4,1)}, u32[]{:S(2)}) copy-start(pred[8]{0:T(512)(128)(4,1)} %compare_and_fusion) | copy-start | bytes 28
  405.7 11.7 %copy-start.29 = (f32[128]{0:T(128)S(1)}, f32[128]{0:T(128)}, u32[]{:S(2)}) copy-start(f32[128]{0:T(128)} %param.21) | copy-start | bytes 1540
  410.8 60.0 %copy-start.13 = (f32[512,64]{1,0:T(8,128)S(1)}, f32[512,64]{1,0:T(8,128)}, u32[]{:S(2)}) copy-start(f32[512,64]{1,0:T(8,128)} %copy-done.12) | copy-start | bytes 393220
  410.8 62.2 %copy-start.9 = (f32[1,512,4,128]{3,2,1,0:T(4,128)S(1)}, f32[1,512,4,128]{3,2,1,0:T(4,128)}, u32[]{:S(2)}) copy-start(f32[1,512,4,128]{3,2,1,0:T(4,128)} %copy-done.8) | copy-start | bytes 3145732
  410.8 54.3 %all-to-all-start.2 = ((bf16[8,512,512]{1,2,0:T(8,128)(2,1)}), bf16[8,512,512]{1,2,0:T(8,128)(2,1)}, u32[]{:S(2)}, u32[]{:S(2)}) async-start(bf16[8,512,512]{1,2,0:T(8,128)(2,1)} %get-tuple-element.215), calls=%async_computation.2 | async-start | bytes 8388608 | tf_op jit(solution)/shard_map/all_to_all | solution.py:259
  416.2 338.3 %reduce-scatter.7.cloned.1.call-start = ((), (), s32[]{:S(2)}) async-start(), calls=%async_computation.8 | async-start | bytes 11141120
  466.2 15.1 %copy-start.7 = (f32[512,512]{0,1:T(8,128)S(1)}, f32[512,512]{0,1:T(8,128)}, u32[]{:S(2)}) copy-start(f32[512,512]{0,1:T(8,128)} %copy-done.6) | copy-start | bytes 3145732
  466.2 15.1 %copy-start.23 = (f32[512,4]{0,1:T(4,128)S(1)}, f32[512,4]{0,1:T(4,128)}, u32[]{:S(2)}) copy-start(f32[512,4]{0,1:T(4,128)} %copy-done.22) | copy-start | bytes 24580
  502.0 254.7 %reduce-scatter.9.cloned.1.call-start = ((), (), s32[]{:S(2)}) async-start(), calls=%async_computation.9 | async-start | bytes 11141120
  577.2 240.7 %all-reduce.4.cloned.1.call-start = ((), (), s32[]{:S(2)}) async-start(), calls=%async_computation.10 | async-start | bytes 3145728 | tf_op jit(solution)/shard_map/psum | solution.py:303
  659.9 21.3 %copy-start.11 = (f32[1,512,4,64]{3,2,1,0:T(4,128)S(1)}, f32[1,512,4,64]{3,2,1,0:T(4,128)}, u32[]{:S(2)}) copy-start(f32[1,512,4,64]{3,2,1,0:T(4,128)} %copy-done.10) | copy-start | bytes 1572868
  659.9 21.3 %copy-start.21 = (f32[2048,128]{1,0:T(8,128)S(1)}, f32[2048,128]{1,0:T(8,128)}, u32[]{:S(2)}) copy-start(f32[2048,128]{1,0:T(8,128)} %reshape.677) | copy-start | bytes 3145732
  (26 other events, 125.4 us)
Sparse Core Ops, SparseCore 0:
  10.2 59.6 all-gather.2
  72.1 56.0 all-gather.4
  502.2 87.0 reduce-scatter.6
  592.5 88.9 reduce-scatter.8
  759.2 58.6 all-reduce.3
where the time goes:
time: 840 us; the launch traced here: 829 us
  waiting for transfers between devices  242 us (29%)
  matrix products  169 us (20%)
  local copies, waits for them, and re-layouts  144 us (17%)
  other arithmetic  121 us (14%)
  blocking collectives  119 us (14%)
  between operations  17.2 us (2%)
  starting transfers between devices  16.2 us (2%)
    unnamed x73, local copies, waits for them, and re-layouts  66.5 us
    psum x1, blocking collectives, per_device(): lax.psum((query_part, key_part), ('dp', 'fsdp'))  64.8 us
    all_to_all x1, blocking collectives, per_device(): lax.all_to_all(pick_tiles(grad_value_pack, back_tile, back_live), 'dp', s...  53.8 us
    all_gather x1, waiting for transfers between devices, per_device(): lax.all_gather(key_weight, 'fsdp', axis=0, tiled=True)  51.6 us
    all_to_all x1, waiting for transfers between devices, per_device(): lax.all_to_all(pick_tiles(grad_key_pack, back_tile, back_live), 'dp', spl...  47.7 us
    psum x1, waiting for transfers between devices, per_device(): lax.psum((key_shard, value_shard), 'dp')  47.6 us
    all_to_all x1, waiting for transfers between devices, per_device(): lax.all_to_all(pick_tiles(key_rot, send_tile, send_live), 'dp', split_axi...  46.9 us
    all_gather x1, waiting for transfers between devices, per_device(): lax.all_gather(value_weight, 'fsdp', axis=0, tiled=True)  46.7 us
  transfers between devices with their start and end apart: 8, of which 6 were waited for; matrix products, arithmetic and copies ran while one was open for 26% of the time, Pallas kernels for 0%

commit v1 on v0

v1 whole, which is shorter than its diff:
```python
import functools
import math

import jax
import jax.numpy as jnp
import numpy as np
from jax import lax
from jax.experimental import pallas as pl
from jax.experimental.pallas import tpu as pltpu
from jax.sharding import PartitionSpec as P

MESH = pl.DeviceIdType.MESH
BF, F32 = jnp.bfloat16, jnp.float32
HD = 128
GSIZE = 4
TILE = 512
D = 5120
KVH = 4
QH = 32
GROUP = QH // KVH
NDP = 8
SHARD = 320
HALF = SHARD // 2
PIECE = TILE // NDP
EPS = 1e-06
VMEM_LIMIT = 60 * 1024 * 1024


def rope_arrays():
    half = HD // 2
    frequency = 1000000.0 ** (-np.arange(half, dtype=np.float64) / half)
    angles = np.arange(TILE, dtype=np.float64)[:, None] * frequency[None, :]
    cosine, sine = np.cos(angles), np.sin(angles)
    return (
        np.concatenate([cosine, cosine], axis=1).astype(np.float32),
        np.concatenate([-sine, sine], axis=1).astype(np.float32),
    )


def place():
    dp, fs = lax.axis_index("dp"), lax.axis_index("fsdp")
    return dp, fs, dp // 2, dp % 2, fs // 4, fs % 4


def remote(src, dst, send, recv, device):
    return pltpu.make_async_remote_copy(
        src_ref=src, dst_ref=dst, send_sem=send, recv_sem=recv, device_id=device, device_id_type=MESH
    )


def entry_barrier(peers):
    barrier = pltpu.get_barrier_semaphore()
    for peer in peers:
        pl.semaphore_signal(barrier, inc=1, device_id=peer, device_id_type=MESH)
    pl.semaphore_wait(barrier, len(peers))


def swap_lanes(values):
    return pltpu.roll(values, HD // 2, axis=1)


class Sends:
    def __init__(self):
        self.pending = []

    def start(self, *args):
        copy = remote(*args)
        copy.start()
        self.pending.append(copy)

    def drain(self):
        for copy in self.pending:
            copy.wait_send()
        self.pending = []


def skewed(stages, chunks, skew=1):
    for tick in range(len(stages) + skew * (chunks - 1)):
        for chunk in range(chunks):
            step = tick - skew * chunk
            if 0 <= step < len(stages):
                stages[step](chunk)


def gather_kernel(
    x_hbm, w_hbm, gain_ref, cos_ref, sin_ref, pick_ref,
    wfull_hbm, kv_hbm, raw_ref, xt_hbm,
    x_v, w_v, xt_v, tile_v, mid0, mid1, mid2, mid3, out_v,
    load_sem, ag_send, ag_recv, ex_send, ex_recv, store_sem,
):
    mids = (mid0, mid1, mid2, mid3)
    dp, fs, cx, core, y, z = place()
    sibling = (dp + 1 - 2 * core, fs)

    def at(dy, dz):
        return (dp, ((y + dy) % 4) * 4 + (z + dz) % 4)

    peers = [((dp + k) % NDP, fs) for k in range(1, NDP)]
    peers += [at(1, 0), at(3, 0), at(0, 1), at(0, 3)]
    load_x = pltpu.make_async_copy(x_hbm, x_v, load_sem.at[KVH])
    load_w = [
        pltpu.make_async_copy(
            w_hbm.at[core, :, pl.ds(h * HD, HD)], w_v.at[core, h, y, z], load_sem.at[h]
        )
        for h in range(KVH)
    ]
    for copy in load_w:
        copy.start()
    load_x.start()
    entry_barrier(peers)
    for copy in load_w:
        copy.wait()
    sends = Sends()

    def block(h, s, d1, d2, low, rows):
        dy, dz = (d1, d2) if s == 0 else (d2, d1)
        return w_v.at[core, h, (y + dy) % 4, (z + dz) % 4, pl.ds(s * HALF + low, rows), :]

    def ahead(s, axis, step):
        return at(step, 0) if (s == 0) == (axis == 1) else at(0, step)

    def pass_on(h, s, axis, step, ref, slot):
        sends.start(ref, ref, ag_send.at[h, s, slot], ag_recv.at[h, s, slot], ahead(s, axis, step))

    def landed(h, s, ref, slot):
        remote(ref, ref, ag_send.at[h, s, slot], ag_recv.at[h, s, slot], sibling).wait_recv()

    quarter = HALF // 2

    def both_ways(h, s, b):
        ref = block(h, s, b, 0, 0, HALF)
        pass_on(h, s, 2, 1, ref, 4 + 4 * b)
        pass_on(h, s, 2, 3, ref, 5 + 4 * b)

    def own(h):
        for s in range(2):
            ref = block(h, s, 0, 0, 0, HALF)
            pass_on(h, s, 1, 1, ref, 0)
            pass_on(h, s, 1, 3, ref, 1)
        for s in range(2):
            both_ways(h, s, 0)

    def near(h):
        for s in range(2):
            landed(h, s, block(h, s, 3, 0, 0, HALF), 0)
            pass_on(h, s, 1, 1, block(h, s, 3, 0, 0, quarter), 2)
            landed(h, s, block(h, s, 1, 0, 0, HALF), 1)
            pass_on(h, s, 1, 3, block(h, s, 1, 0, quarter, quarter), 3)
        for s in range(2):
            both_ways_from(h, s)

    def both_ways_from(h, s):
        for b in (3, 1):
            both_ways(h, s, b)

    def far(h):
        for s in range(2):
            landed(h, s, block(h, s, 2, 0, 0, quarter), 2)
            landed(h, s, block(h, s, 2, 0, quarter, quarter), 3)
            both_ways(h, s, 2)

    def relay(h, blocks):
        for b in blocks:
            for s in range(2):
                landed(h, s, block(h, s, b, 3, 0, HALF), 4 + 4 * b)
                pass_on(h, s, 2, 1, block(h, s, b, 3, 0, quarter), 6 + 4 * b)
                landed(h, s, block(h, s, b, 1, 0, HALF), 5 + 4 * b)
                pass_on(h, s, 2, 3, block(h, s, b, 1, quarter, quarter), 7 + 4 * b)

    def share(h):
        for b in (0, 3, 1, 2):
            for s in range(2):
                landed(h, s, block(h, s, b, 2, 0, quarter), 6 + 4 * b)
                landed(h, s, block(h, s, b, 2, quarter, quarter), 7 + 4 * b)
        sends.start(
            w_v.at[core, h], w_v.at[core, h], ex_send.at[h, 0, 0], ex_recv.at[h, 0, 0], sibling
        )

    stores = []

    def project(h):
        other = w_v.at[1 - core, h]
        remote(other, other, ex_send.at[h, 0, 0], ex_recv.at[h, 0, 0], sibling).wait_recv()
        for c in range(2):
            copy = pltpu.make_async_copy(w_v.at[c, h], wfull_hbm.at[c, h], store_sem.at[2 * h + c])
            copy.start()
            stores.append(copy)

        @pl.loop(0, 2)
        def _(part):
            rows = pl.ds(pl.multiple_of(part * 256, 256), 256)
            weights = jnp.concatenate(
                [w_v[0, h].reshape(D, HD), w_v[1, h].reshape(D, HD)], axis=1
            )
            both = jnp.dot(x_v[rows, :], weights, preferred_element_type=F32)
            raw = both[:, :HD]
            raw_ref[h, rows, :] = raw
            scale = lax.rsqrt(jnp.mean(raw * raw, axis=1, keepdims=True) + EPS)
            normed = raw * scale * gain_ref[...]
            rot = normed * cos_ref[rows, :] + swap_lanes(normed) * sin_ref[rows, :]
            tile_v[h, rows, :] = jnp.concatenate([rot, both[:, HD:]], axis=1).astype(BF)

        for k in range(1, NDP):
            to = (dp + k) % NDP
            sends.start(
                tile_v.at[h, pl.ds(to * PIECE, PIECE), :], mids[h].at[dp],
                ex_send.at[h, 0, k], ex_recv.at[h, 0, k], (to, fs),
            )
        mids[h][dp] = tile_v[h, pl.ds(pl.multiple_of(dp * PIECE, PIECE), PIECE), :]

    def forward(h):
        for k in range(1, NDP):
            ref = mids[h].at[(dp + NDP - k) % NDP]
            remote(ref, ref, ex_send.at[h, 0, k], ex_recv.at[h, 0, k], sibling).wait_recv()
        for k in range(NDP):
            to = (dp + k) % NDP
            out_v[h, k] = mids[h][pick_ref[to]]
            ref = kv_hbm.at[h, pl.ds(dp * PIECE, PIECE), :]
            if k == 0:
                copy = pltpu.make_async_copy(out_v.at[h, k], ref, store_sem.at[2 * KVH + h])
                copy.start()
                stores.append(copy)
            else:
                sends.start(
                    out_v.at[h, k], ref, ex_send.at[h, 1, k], ex_recv.at[h, 1, k], (to, fs)
                )

    def arrive(h):
        for k in range(1, NDP):
            ref = kv_hbm.at[h, pl.ds(((dp + NDP - k) % NDP) * PIECE, PIECE), :]
            remote(ref, ref, ex_send.at[h, 1, k], ex_recv.at[h, 1, k], sibling).wait_recv()

    def turn(h):
        if h == 0:
            load_x.wait()

        step = D // KVH

        @pl.loop(0, step // 256)
        def _(part):
            start = pl.multiple_of(h * step + part * 256, 256)
            xt_v[pl.ds(start, 256), :] = x_v[:, pl.ds(start, 256)].T

        copy = pltpu.make_async_copy(
            xt_v.at[pl.ds(h * step, step)], xt_hbm.at[pl.ds(h * step, step)],
            store_sem.at[3 * KVH + h],
        )
        copy.start()
        stores.append(copy)

    def relay_early(h):
        relay(h, (0, 3, 1))

    def relay_late(h):
        relay(h, (2,))

    def near_turn(h):
        near(h)
        turn(h)

    stages = [own, near_turn, far, relay_early, relay_late, share, project, forward, arrive]
    skewed(stages, KVH)
    sends.drain()
    for copy in stores:
        copy.wait()


def gather_call(x, weights, gain, cosine, sine, pick):
    any_spec = pl.BlockSpec(memory_space=pl.ANY)
    vmem_spec = pl.BlockSpec(memory_space=pltpu.VMEM)
    return pl.pallas_call(
        gather_kernel,
        out_shape=(
            jax.ShapeDtypeStruct((2, KVH, 4, 4, SHARD, HD), BF),
            jax.ShapeDtypeStruct((KVH, TILE, 2 * HD), BF),
            jax.ShapeDtypeStruct((KVH, TILE, HD), F32),
            jax.ShapeDtypeStruct((D, TILE), BF),
        ),
        in_specs=[any_spec, any_spec, vmem_spec, vmem_spec, vmem_spec,
                  pl.BlockSpec(memory_space=pltpu.SMEM)],
        out_specs=(any_spec, any_spec, vmem_spec, any_spec),
        scratch_shapes=[
            pltpu.VMEM((TILE, D), BF),
            pltpu.VMEM((2, KVH, 4, 4, SHARD, HD), BF),
            pltpu.VMEM((D, TILE), BF),
            pltpu.VMEM((KVH, TILE, 2 * HD), BF),
            *[pltpu.VMEM((NDP, PIECE, 2 * HD), BF)] * KVH,
            pltpu.VMEM((KVH, NDP, PIECE, 2 * HD), BF),
            pltpu.SemaphoreType.DMA((KVH + 1,)),
            pltpu.SemaphoreType.DMA((KVH, 2, 20)),
            pltpu.SemaphoreType.DMA((KVH, 2, 20)),
            pltpu.SemaphoreType.DMA((KVH, 2, NDP)),
            pltpu.SemaphoreType.DMA((KVH, 2, NDP)),
            pltpu.SemaphoreType.DMA((4 * KVH,)),
        ],
        compiler_params=pltpu.CompilerParams(
            collective_id=0, has_side_effects=True, vmem_limit_bytes=VMEM_LIMIT
        ),
        name="gather_project_send",
    )(x, weights, gain, cosine, sine, pick)


def attention_kernel(
    q_ref, og_ref, kv_ref, gain_ref, cos_ref, sin_ref, coef_ref,
    dq_ref, gkv_ref, gq_ref,
    kt_v, vt_v, va_v, acc_k, acc_v, acc_gain,
):
    step = pl.program_id(0)
    inner = step % GROUP

    @pl.when(step == 0)
    def _():
        acc_gain[...] = jnp.zeros_like(acc_gain)

    @pl.when(inner == 0)
    def _():
        keys, values = kv_ref[0, :, :HD], kv_ref[0, :, HD:]
        ones = jnp.ones((TILE, HD), BF)
        kt_v[...] = keys.T
        vt_v[:HD, :] = values.T
        vt_v[HD:, :] = jnp.ones((HD, TILE), BF)
        va_v[:, :HD] = values
        va_v[:, HD:] = ones
        acc_k[...] = jnp.zeros_like(acc_k)
        acc_v[...] = jnp.zeros_like(acc_v)

    half = HD // 2

    def swap(values):
        return jnp.concatenate([values[half:], values[:half]], axis=0)

    cosine, sine, gain = cos_ref[...], sin_ref[...], gain_ref[...]
    raw = q_ref[...].astype(F32).T
    scale = lax.rsqrt(jnp.mean(raw * raw, axis=0, keepdims=True) + EPS)
    unit = raw * scale
    normed = unit * gain
    rot = normed * cosine + swap(normed) * sine
    query = (rot * (math.log2(math.e) / math.sqrt(HD))).astype(BF)
    weighted = (og_ref[...].astype(F32).T * coef_ref[...]).astype(BF).astype(F32)

    contract_lanes = (((1,), (1,)), ((), ()))
    row = lax.broadcasted_iota(jnp.int32, (256, 256), 0)
    lane = lax.broadcasted_iota(jnp.int32, (256, 256), 1)
    causal = row <= lane
    sub = lax.broadcasted_iota(jnp.int32, (HD, 256), 0)
    grads = []
    for ib in range(2):
        cols = slice(ib * 256, ib * 256 + 256)
        seen = ib * 256 + 256
        qb = query[:, cols]
        scores = jnp.dot(kv_ref[0, :seen, :HD], qb, preferred_element_type=F32)
        weight = jnp.exp2(scores)
        last = jnp.where(causal, weight[ib * 256:], 0.0)
        weight = last if ib == 0 else jnp.concatenate([weight[:256], last], axis=0)
        low = weight.astype(BF)
        sums = jnp.dot(vt_v[:, :seen], low, preferred_element_type=F32)
        inverse = 1.0 / sums[HD:]
        attended = sums[:HD] * inverse
        scaled = (weighted[:, cols] * inverse).astype(BF)
        dotted = jnp.sum(scaled.astype(F32) * attended, axis=0, keepdims=True)
        high = dotted.astype(BF).astype(F32)
        rest = dotted - high
        tail = jnp.where(sub == 0, -high, jnp.where(sub == 1, -rest, 0.0)).astype(BF)
        grad_probs = jnp.dot(
            va_v[:seen, :], jnp.concatenate([scaled, tail], axis=0), preferred_element_type=F32
        )
        grad_scores = (weight * grad_probs).astype(BF)
        acc_v[:seen, :] += lax.dot_general(low, scaled, contract_lanes, preferred_element_type=F32)
        acc_k[:seen, :] += lax.dot_general(
            grad_scores, qb, contract_lanes, preferred_element_type=F32
        )
        grads.append(jnp.dot(kt_v[:, :seen], grad_scores, preferred_element_type=F32))
    grad_rot = jnp.concatenate(grads, axis=1) * (1.0 / math.sqrt(HD))
    grad_normed = grad_rot * cosine - swap(grad_rot) * sine
    terms = grad_normed * unit
    acc_gain[...] += terms[:, :128] + terms[:, 128:256] + terms[:, 256:384] + terms[:, 384:]
    mean = jnp.mean(terms * gain, axis=0, keepdims=True)
    dq_ref[...] = (scale * (grad_normed * gain - unit * mean)).T.astype(BF)

    @pl.when(inner == GROUP - 1)
    def _():
        gkv_ref[0, :, :HD] = (acc_k[...] * math.log(2.0)).astype(BF)
        gkv_ref[0, :, HD:] = acc_v[...].astype(BF)

    @pl.when(step == QH - 1)
    def _():
        gq_ref[...] = jnp.sum(acc_gain[...].T, axis=0, keepdims=True)


def attention_call(queries, out_grad, kv, gain, cosine, sine, coef):
    head_spec = pl.BlockSpec((TILE, HD), lambda n: (0, n))
    kv_spec = pl.BlockSpec((1, TILE, 2 * HD), lambda n: (n // GROUP, 0, 0))
    whole = lambda shape: pl.BlockSpec(shape, lambda n: (0, 0))
    return pl.pallas_call(
        attention_kernel,
        grid=(QH,),
        out_shape=(
            jax.ShapeDtypeStruct((TILE, QH * HD), BF),
            jax.ShapeDtypeStruct((KVH, TILE, 2 * HD), BF),
            jax.ShapeDtypeStruct((1, HD), F32),
        ),
        in_specs=[head_spec, head_spec, kv_spec, whole((HD, TILE)), whole((HD, TILE)),
                  whole((HD, TILE)), whole((1, TILE))],
        out_specs=(head_spec, kv_spec, whole((1, HD))),
        scratch_shapes=[
            pltpu.VMEM((HD, TILE), BF),
            pltpu.VMEM((2 * HD, TILE), BF),
            pltpu.VMEM((TILE, 2 * HD), BF),
            pltpu.VMEM((TILE, HD), F32),
            pltpu.VMEM((TILE, HD), F32),
            pltpu.VMEM((HD, HD), F32),
        ],
        compiler_params=pltpu.CompilerParams(vmem_limit_bytes=VMEM_LIMIT),
        name="attention_both_ways",
    )(queries, out_grad, kv, gain, cosine, sine, coef)


def reduce_kernel(
    gkv_hbm, xt_hbm, raw_ref, gq_ref, gain_ref, cos_ref, sin_ref, pick_ref,
    g_ref, outk_ref, outv_ref, gain_out,
    xt_v, mid0, mid1, mid2, mid3, pass_v, back_v, dw_v, pair_v, r1_v, r2_v, q_v, r4_v, r5_v, f_v, r7_v, full_v,
    gain_v, gain_r,
    load_sem, ex_send, ex_recv, rs_send, rs_recv, x_send, x_recv, gn_send, gn_recv,
):
    mids = (mid0, mid1, mid2, mid3)
    dp, fs, cx, core, y, z = place()
    sibling = (dp + 1 - 2 * core, fs)

    def at(dy, dz):
        return (dp, ((y + dy) % 4) * 4 + (z + dz) % 4)

    peers = [((dp + k) % NDP, fs) for k in range(1, NDP)]
    peers += [at(k, 0) for k in range(1, 4)] + [at(0, k) for k in range(1, 4)]
    load_x = pltpu.make_async_copy(xt_hbm, xt_v, load_sem.at[0])
    load_x.start()
    own_copies = []
    for h in range(KVH):
        copy = pltpu.make_async_copy(
            gkv_hbm.at[h, pl.ds(dp * PIECE, PIECE), :], mids[h].at[dp], load_sem.at[1 + h]
        )
        copy.start()
        own_copies.append(copy)
    entry_barrier(peers)
    sends = Sends()

    def spread(h):
        for k in range(1, NDP):
            to = (dp + k) % NDP
            sends.start(
                gkv_hbm.at[h, pl.ds(to * PIECE, PIECE), :], mids[h].at[dp],
                ex_send.at[h, 0, k], ex_recv.at[h, 0, k], (to, fs),
            )

    def forward(h):
        own_copies[h].wait()
        for k in range(1, NDP):
            ref = mids[h].at[(dp + NDP - k) % NDP]
            remote(ref, ref, ex_send.at[h, 0, k], ex_recv.at[h, 0, k], sibling).wait_recv()
        for k in range(NDP):
            to = (dp + k) % NDP
            if k == 0:
                back_v[h, dp] = mids[h][pick_ref[to]]
            else:
                pass_v[h, k] = mids[h][pick_ref[to]]
                sends.start(
                    pass_v.at[h, k], back_v.at[h, dp],
                    ex_send.at[h, 1, k], ex_recv.at[h, 1, k], (to, fs),
                )

    gain_parts = []

    def multiply(h):
        if h == 0:
            load_x.wait()
        for k in range(1, NDP):
            ref = back_v.at[h, (dp + NDP - k) % NDP]
            remote(ref, ref, ex_send.at[h, 1, k], ex_recv.at[h, 1, k], sibling).wait_recv()
        grads = back_v[h].reshape(TILE, 2 * HD)
        grad_rot = grads[:, :HD].astype(F32)
        raw = raw_ref[h]
        scale = lax.rsqrt(jnp.mean(raw * raw, axis=1, keepdims=True) + EPS)
        unit = raw * scale
        normed = grad_rot * cos_ref[...] - swap_lanes(grad_rot) * sin_ref[...]
        terms = normed * unit
        gain_parts.append(jnp.sum(terms, axis=0, keepdims=True))
        gained = normed * gain_ref[...]
        mean = jnp.mean(gained * unit, axis=1, keepdims=True)
        g_ref[h, :, :HD] = (scale * (gained - unit * mean)).astype(BF)
        g_ref[h, :, HD:] = grads[:, HD:]

        @pl.loop(0, 16)
        def _(shard):
            sy, sz = shard // 4, shard % 4
            start = pl.multiple_of(shard * SHARD, SHARD)
            part = jnp.dot(xt_v[pl.ds(start, SHARD), :], g_ref[h], preferred_element_type=F32)
            part = part.astype(BF)
            for c in range(2):
                dw_v[h, c, 0, sz, sy] = part[:HALF, c * HD:(c + 1) * HD]
                dw_v[h, c, 1, sy, sz] = part[HALF:, c * HD:(c + 1) * HD]

        for s in range(2):
            sends.start(
                dw_v.at[h, 1 - core, s], pair_v.at[h, s],
                rs_send.at[h, s, 0], rs_recv.at[h, s, 0], sibling,
            )

    def me(s, axis):
        return z if (s == 0) == (axis == 1) else y

    def ahead(s, axis, step):
        return at(0, step) if (s == 0) == (axis == 1) else at(step, 0)

    def send(h, s, slot, src, dst, axis, step):
        sends.start(src, dst, rs_send.at[h, s, slot], rs_recv.at[h, s, slot], ahead(s, axis, step))

    def landed(h, s, slot, ref):
        remote(ref, ref, rs_send.at[h, s, slot], rs_recv.at[h, s, slot], sibling).wait_recv()

    def add(ref, *others):
        total = ref[...].astype(F32)
        for other in others:
            total = total + other[...].astype(F32)
        ref[...] = total.astype(BF)

    def pair(h):
        for s in range(2):
            landed(h, s, 0, pair_v.at[h, s])
            mine = dw_v.at[h, core, s]
            far = (me(s, 1) + 2) % 4
            add(mine.at[far], pair_v.at[h, s, far])
            send(h, s, 1, mine.at[far, 0:2], r1_v.at[h, s, 0], 1, 1)
            send(h, s, 2, mine.at[far, 2:4], r1_v.at[h, s, 1], 1, 3)
        for s in range(2):
            mine = dw_v.at[h, core, s]
            for step in (1, 3, 0):
                index = (me(s, 1) + step) % 4
                add(mine.at[index], pair_v.at[h, s, index])

    def near(h):
        for s in range(2):
            mine = dw_v.at[h, core, s]
            up, down = (me(s, 1) + 1) % 4, (me(s, 1) + 3) % 4
            landed(h, s, 1, r1_v.at[h, s, 0])
            add(mine.at[up, 0:2], r1_v.at[h, s, 0])
            send(h, s, 3, mine.at[up], r2_v.at[h, s, 0], 1, 1)
            landed(h, s, 2, r1_v.at[h, s, 1])
            add(mine.at[down, 2:4], r1_v.at[h, s, 1])
            send(h, s, 4, mine.at[down], r2_v.at[h, s, 1], 1, 3)

    quarter = HALF // 2

    def cross(h):
        for s in range(2):
            landed(h, s, 3, r2_v.at[h, s, 0])
            landed(h, s, 4, r2_v.at[h, s, 1])
            own = dw_v[h, core, s, me(s, 1)].astype(F32)
            q_v[h, s] = (own + r2_v[h, s, 0].astype(F32) + r2_v[h, s, 1].astype(F32)).astype(BF)
            far = (me(s, 2) + 2) % 4
            send(h, s, 5, q_v.at[h, s, far, 0:quarter], r4_v.at[h, s, 0], 2, 1)
            send(h, s, 6, q_v.at[h, s, far, quarter:HALF], r4_v.at[h, s, 1], 2, 3)

    def near_cross(h):
        for s in range(2):
            up, down = (me(s, 2) + 1) % 4, (me(s, 2) + 3) % 4
            landed(h, s, 5, r4_v.at[h, s, 0])
            add(q_v.at[h, s, up, 0:quarter], r4_v.at[h, s, 0])
            send(h, s, 7, q_v.at[h, s, up], r5_v.at[h, s, 0], 2, 1)
            landed(h, s, 6, r4_v.at[h, s, 1])
            add(q_v.at[h, s, down, quarter:HALF], r4_v.at[h, s, 1])
            send(h, s, 8, q_v.at[h, s, down], r5_v.at[h, s, 1], 2, 3)

    def along_x(h):
        for s in range(2):
            landed(h, s, 7, r5_v.at[h, s, 0])
            landed(h, s, 8, r5_v.at[h, s, 1])
            own = q_v[h, s, me(s, 2)].astype(F32)
            f_v[h, s * HALF:(s + 1) * HALF] = (
                own + r5_v[h, s, 0].astype(F32) + r5_v[h, s, 1].astype(F32)
            ).astype(BF)
        for k in range(1, 4):
            to = (cx + k) % 4
            sends.start(
                f_v.at[h, pl.ds(to * 80, 80), :], r7_v.at[h, k - 1],
                x_send.at[h, k - 1], x_recv.at[h, k - 1], (to * 2 + core, fs),
            )

    def spread_x(h):
        for k in range(1, 4):
            ref = r7_v.at[h, k - 1]
            remote(ref, ref, x_send.at[h, k - 1], x_recv.at[h, k - 1], sibling).wait_recv()
        rows = pl.ds(pl.multiple_of(cx * 80, 80), 80)
        total = f_v[h, rows, :].astype(F32)
        for k in range(3):
            total = total + r7_v[h, k].astype(F32)
        full_v[h, core, rows, :] = total.astype(BF)
        for k in range(1, NDP):
            ref = full_v.at[h, core, rows, :]
            sends.start(ref, ref, x_send.at[h, 2 + k], x_recv.at[h, 2 + k], ((dp + k) % NDP, fs))

    def finish(h):
        for k in range(1, NDP):
            source = (dp + NDP - k) % NDP
            ref = full_v.at[h, source % 2, pl.ds((source // 2) * 80, 80), :]
            remote(ref, ref, x_send.at[h, 2 + k], x_recv.at[h, 2 + k], sibling).wait_recv()
        outk_ref[:, h * HD:(h + 1) * HD] = full_v[h, 0].astype(F32)
        outv_ref[:, h * HD:(h + 1) * HD] = full_v[h, 1].astype(F32)

    groups = [
        (0, [((dp + k) % NDP, fs) for k in range(1, NDP)]),
        (7, [at(k, 0) for k in range(1, 4)]),
        (10, [at(0, k) for k in range(1, 4)]),
    ]

    def gains_out(stage):
        base, targets = groups[stage]
        for k, target in enumerate(targets):
            sends.start(
                gain_v.at[stage], gain_r.at[base + k], gn_send.at[base + k], gn_recv.at[base + k],
                target,
            )

    def gains_in(stage):
        base, targets = groups[stage]
        total = gain_v[stage]
        for k in range(len(targets)):
            ref = gain_r.at[base + k]
            remote(ref, ref, gn_send.at[base + k], gn_recv.at[base + k], sibling).wait_recv()
            total = total + gain_r[base + k]
        gain_v[stage + 1] = total

    def gains(stage):
        if stage == 0:
            row = lax.broadcasted_iota(jnp.int32, (8, HD), 0)
            keys = gain_parts[0] + gain_parts[1] + gain_parts[2] + gain_parts[3]
            gain_v[0] = jnp.where(row == 0, gq_ref[...], jnp.where(row == 1, keys, 0.0))
        else:
            gains_in(stage - 1)
        if stage < 3:
            gains_out(stage)
        else:
            gain_out[...] = gain_v[3]

    def then_gains(stage_function, stage):
        def both(h):
            stage_function(h)
            if h == KVH - 1:
                gains(stage)

        return both

    stages = [
        spread, forward, then_gains(multiply, 0), pair, then_gains(near, 1), then_gains(cross, 2),
        then_gains(near_cross, 3), along_x, spread_x, finish,
    ]
    skewed(stages, KVH)
    sends.drain()


def reduce_call(gkv, xt, raw, gq, gain, cosine, sine, pick):
    any_spec = pl.BlockSpec(memory_space=pl.ANY)
    vmem_spec = pl.BlockSpec(memory_space=pltpu.VMEM)
    return pl.pallas_call(
        reduce_kernel,
        out_shape=(
            jax.ShapeDtypeStruct((KVH, TILE, 2 * HD), BF),
            jax.ShapeDtypeStruct((SHARD, KVH * HD), F32),
            jax.ShapeDtypeStruct((SHARD, KVH * HD), F32),
            jax.ShapeDtypeStruct((8, HD), F32),
        ),
        in_specs=[any_spec, any_spec] + [vmem_spec] * 5 + [pl.BlockSpec(memory_space=pltpu.SMEM)],
        out_specs=(vmem_spec,) * 4,
        scratch_shapes=[
            pltpu.VMEM((D, TILE), BF),
            *[pltpu.VMEM((NDP, PIECE, 2 * HD), BF)] * KVH,
            pltpu.VMEM((KVH, NDP, PIECE, 2 * HD), BF),
            pltpu.VMEM((KVH, NDP, PIECE, 2 * HD), BF),
            pltpu.VMEM((KVH, 2, 2, 4, 4, HALF, HD), BF),
            pltpu.VMEM((KVH, 2, 4, 4, HALF, HD), BF),
            pltpu.VMEM((KVH, 2, 2, 2, HALF, HD), BF),
            pltpu.VMEM((KVH, 2, 2, 4, HALF, HD), BF),
            pltpu.VMEM((KVH, 2, 4, HALF, HD), BF),
            pltpu.VMEM((KVH, 2, 2, HALF // 2, HD), BF),
            pltpu.VMEM((KVH, 2, 2, HALF, HD), BF),
            pltpu.VMEM((KVH, SHARD, HD), BF),
            pltpu.VMEM((KVH, 3, 80, HD), BF),
            pltpu.VMEM((KVH, 2, SHARD, HD), BF),
            pltpu.VMEM((4, 8, HD), F32),
            pltpu.VMEM((13, 8, HD), F32),
            pltpu.SemaphoreType.DMA((KVH + 1,)),
            pltpu.SemaphoreType.DMA((KVH, 2, NDP)),
            pltpu.SemaphoreType.DMA((KVH, 2, NDP)),
            pltpu.SemaphoreType.DMA((KVH, 2, 9)),
            pltpu.SemaphoreType.DMA((KVH, 2, 9)),
            pltpu.SemaphoreType.DMA((KVH, 10)),
            pltpu.SemaphoreType.DMA((KVH, 10)),
            pltpu.SemaphoreType.DMA((13,)),
            pltpu.SemaphoreType.DMA((13,)),
        ],
        compiler_params=pltpu.CompilerParams(
            collective_id=1, has_side_effects=True, vmem_limit_bytes=VMEM_LIMIT
        ),
        name="return_multiply_reduce",
    )(gkv, xt, raw, gq, gain, cosine, sine, pick)


def hidden_kernel(g_ref, w_ref, out_ref):
    grads = jnp.concatenate(
        [g_ref[h, :, c * HD:(c + 1) * HD] for h in range(KVH) for c in range(2)], axis=1
    )
    weights = jnp.concatenate([w_ref[c, h] for h in range(KVH) for c in range(2)], axis=1)
    out_ref[...] = lax.dot_general(
        grads, weights, (((1,), (1,)), ((), ())), preferred_element_type=F32
    ).astype(BF)


def hidden_call(g, weights):
    block = 512
    return pl.pallas_call(
        hidden_kernel,
        grid=(D // block,),
        out_shape=jax.ShapeDtypeStruct((TILE, D), BF),
        in_specs=[
            pl.BlockSpec((KVH, TILE, 2 * HD), lambda n: (0, 0, 0)),
            pl.BlockSpec((2, KVH, block, HD), lambda n: (0, 0, n, 0)),
        ],
        out_specs=pl.BlockSpec((TILE, block), lambda n: (0, n)),
        compiler_params=pltpu.CompilerParams(vmem_limit_bytes=VMEM_LIMIT),
        name="hidden_gradient",
    )(g, weights)


def per_device(
    rollout_hidden, key_weight, value_weight, key_gain, query_gain, queries, out_grad, rewards,
    response_lengths, rollout_owner, train_shard, pack_offsets,
):
    del pack_offsets
    dp = lax.axis_index("dp")
    lengths, owners, trainers = response_lengths[0], rollout_owner[0], train_shard[0]
    index = jnp.arange(NDP, dtype=jnp.int32)
    by_trainer = (trainers[None, :] == index[:, None]).astype(jnp.int32)
    by_owner = (owners[None, :] == index[:, None]).astype(jnp.int32)
    owner_of = jnp.sum(by_trainer * owners[None, :], axis=1)
    trainer_of = jnp.sum(by_owner * trainers[None, :], axis=1)
    grouped = rewards[0].reshape(-1, GSIZE)
    advantage = (grouped - jnp.mean(grouped, axis=-1, keepdims=True)).reshape(-1)
    mine = trainers == dp
    length = jnp.sum(jnp.where(mine, lengths, 0))
    factor = jnp.sum(jnp.where(mine, advantage, 0.0))
    coef = jnp.where(jnp.arange(TILE) < length, factor, 0.0).reshape(1, TILE)

    cosine, sine = rope_arrays()
    key_gain_row = key_gain.reshape(1, HD)
    query_gain_wide = jnp.broadcast_to(query_gain[:, None], (HD, TILE))
    weights = jnp.stack([key_weight, value_weight])
    full, kv, raw, xt = gather_call(
        rollout_hidden, weights, key_gain_row, cosine, sine, owner_of
    )
    d_queries, gkv, gq = attention_call(
        queries, out_grad, kv, query_gain_wide,
        np.ascontiguousarray(cosine.T), np.ascontiguousarray(sine.T), coef,
    )
    g, grad_key_weight, grad_value_weight, gains = reduce_call(
        gkv, xt, raw, gq, key_gain_row, cosine, sine, trainer_of
    )
    d_hidden = hidden_call(g, full.reshape(2, KVH, D, HD))
    return d_hidden, d_queries, grad_key_weight, grad_value_weight, gains[0], gains[1]


def solution(mesh):
    rows, split = P(("dp", "fsdp"), None), P("fsdp", None)
    return jax.shard_map(
        per_device,
        mesh=mesh,
        in_specs=(rows, split, split, P(), P(), rows, rows, split, split, split, split, split),
        out_specs=(rows, rows, split, split, P(), P()),
        check_vma=False,
    )
```

time: 840 us -> 253 us (0.30); the launches traced: 829 us -> 253 us
  waiting for transfers between devices: 242 us -> 0 us
  Pallas kernels: 0 us -> 238 us
  matrix products: 169 us -> 0 us
  local copies, waits for them, and re-layouts: 144 us -> 5.14 us
  blocking collectives: 119 us -> 0 us
  other arithmetic: 121 us -> 9.22 us
  between operations: 17.2 us -> 0.68 us
  starting transfers between devices: 16.2 us -> 0 us
    pallas_call x0 -> x4, Pallas kernels: none -> 238 us  [the longest x1 84.3 us: reduce_call(): pl.pallas_call(reduce_kernel, out_shape=(jax.ShapeDtypeStruct((KVH, TILE,...]
    dot_general x30 -> x0, matrix products: 169 us -> none  [the longest x4 26.3 us: attend_head(): jnp.einsum('bigd,bjd->bgij', query_rot, key_tiles, preferred_element_type...]
    all_gather x2 -> x0, waiting for transfers between devices: 98.3 us -> none  [the longest x1 51.6 us: per_device(): lax.all_gather(key_weight, 'fsdp', axis=0, tiled=True)]
    all_to_all x3 -> x0, waiting for transfers between devices: 94.8 us -> none  [the longest x1 47.7 us: per_device(): lax.all_to_all(pick_tiles(grad_key_pack, back_tile, back_live), 'dp', spl...]
    psum x1 -> x0, blocking collectives: 64.8 us -> none  [per_device(): lax.psum((query_part, key_part), ('dp', 'fsdp'))]
    unnamed x73 -> x7, local copies, waits for them, and re-layouts: 66.5 us -> 2.19 us
    all_to_all x1 -> x0, blocking collectives: 53.8 us -> none  [per_device(): lax.all_to_all(pick_tiles(grad_value_pack, back_tile, back_live), 'dp', s...]
    psum x1 -> x0, waiting for transfers between devices: 47.6 us -> none  [per_device(): lax.psum((key_shard, value_shard), 'dp')]
  transfers between devices with their start and end apart: 8 -> 0, of which waited for: 6 -> 0; matrix products, arithmetic and copies ran while one was open for 26% -> 0% of each run, Pallas kernels for 0% -> 0%
where the time goes in v1:
time: 253 us
  Pallas kernels  238 us (94%)
  other arithmetic  9.22 us (4%)
  local copies, waits for them, and re-layouts  5.14 us (2%)
    pallas_call x1, Pallas kernels, reduce_call(): pl.pallas_call(reduce_kernel, out_shape=(jax.ShapeDtypeStruct((KVH, TILE,...  84.3 us
    pallas_call x1, Pallas kernels, gather_call(): pl.pallas_call(gather_kernel, out_shape=(jax.ShapeDtypeStruct((2, KVH, 4,...  76.6 us
    pallas_call x1, Pallas kernels, attention_call(): pl.pallas_call(attention_kernel, grid=(QH,), out_shape=(jax.ShapeDtypeStr...  63.9 us
    pallas_call x1, Pallas kernels, hidden_call(): pl.pallas_call(hidden_kernel, grid=(D // block,), out_shape=jax.ShapeDtyp...  13 us

profile of v1, /device:TPU:1, one launch (start us, length us, event | category | flops | bytes accessed | tf_op | source)
XLA Modules:
  0.0 252.8 jit_solution(18252607434681651116)
XLA Ops:
  0.6 0.5 broadcast.44
  1.1 1.3 reduce.3
  2.5 1.3 fusion
  3.8 0.1 reshape_squeeze.6
  3.9 0.1 reduce_sum.47
  4.0 0.1 sub.11
  4.1 0.1 sub.12
  4.1 1.3 fusion.1
  5.4 1.9 compare_select_fusion.coef_ref
  7.3 1.3 select_reduce_fusion
  8.6 1.4 broadcast_in_dim.25.gain_ref
  10.1 2.0 pad_maximum_fusion.w_hbm
  12.1 76.6 %gather_project_send.1 = (bf16[2,4,4,4,320,128]{5,4,3,2,1,0:T(8,128)(2,1)}, bf16[4,512,256]{2,1,0:T(8,128)(2,1)}, f32[4,512,128]{2,1,0:T(8,128)}, bf16[5120,512]{1,0:T(8,128)(2,1)}) custom-call(bf16[512,5120]{1,0:T(8,128)(2,1)} %x_hbm.1, bf16[2,320,512]{2,1,0:T(8,128)(2,1)} %pad_maximum_fusion.w_hbm, f32[1,128]{1,0:T(1,128)} %bitcast.22, ...), custom_call_target="tpu_custom_call" | custom-call | tf_op jit(solution)/shard_map/gather_project_send/pallas_call | solution.py:271
  88.7 63.9 %attention_both_ways.1 = (bf16[512,4096]{1,0:T(8,128)(2,1)}, bf16[4,512,256]{2,1,0:T(8,128)(2,1)}, f32[1,128]{1,0:T(1,128)}) custom-call(bf16[512,4096]{1,0:T(8,128)(2,1)} %q_ref.1, bf16[512,4096]{1,0:T(8,128)(2,1)} %og_ref.1, bf16[4,512,256]{2,1,0:T(8,128)(2,1)} %get-tuple-element.17.kv_ref, f32[128,512]{1,0:T(8,128)} %broadcast_in_dim.25.gain_ref, ...), custom_call_target="tpu_custom_call" | custom-call | tf_op jit(solution)/shard_map/attention_both_ways/pallas_call | solution.py:394
  152.6 84.3 %return_multiply_reduce.1 = (bf16[4,512,256]{2,1,0:T(8,128)(2,1)}, f32[320,512]{1,0:T(8,128)}, f32[320,512]{1,0:T(8,128)}, f32[8,128]{1,0:T(8,128)}) custom-call(bf16[4,512,256]{2,1,0:T(8,128)(2,1)} %get-tuple-element.18.gkv_hbm, bf16[5120,512]{1,0:T(8,128)(2,1)} %get-tuple-element.19.xt_hbm, f32[4,512,128]{2,1,0:T(8,128)} %get-tuple-element.20.raw_ref, ...), custom_call_target="tpu_custom_call" | custom-call | tf_op jit(solution)/shard_map/return_multiply_reduce/pallas_call | solution.py:662
  236.9 0.0 copy-start.1
  236.9 0.0 copy-start
  236.9 13.0 %hidden_gradient.1 = bf16[512,5120]{1,0:T(8,128)(2,1)} custom-call(bf16[4,512,256]{2,1,0:T(8,128)(2,1)} %get-tuple-element.22.g_ref, bf16[2,4,5120,128]{3,2,1,0:T(8,128)(2,1)} %bitcast.18), custom_call_target="tpu_custom_call" | custom-call | tf_op jit(solution)/shard_map/hidden_gradient/pallas_call | solution.py:718
  249.8 1.3 slice_bitcast_fusion
  251.1 0.0 copy-done.1
  251.1 0.8 copy.23
  251.9 0.0 copy-done
  252.0 0.8 copy.24
  (1 shorter events, 0.0 us)
Async XLA Ops:
  236.9 14.2 %copy-start.1 = (f32[320,512]{1,0:T(8,128)S(1)}, f32[320,512]{1,0:T(8,128)}, u32[]{:S(2)}) copy-start(f32[320,512]{1,0:T(8,128)} %get-tuple-element.40) | copy-start | bytes 1966084
  236.9 15.1 %copy-start = (f32[320,512]{1,0:T(8,128)S(1)}, f32[320,512]{1,0:T(8,128)}, u32[]{:S(2)}) copy-start(f32[320,512]{1,0:T(8,128)} %get-tuple-element.41) | copy-start | bytes 1966084
